TPU v7x, 512 devices: a whole 4x4x16 slice. The times are simulated.
512 devices in a mesh: ctx: 64 (over y, z), exp: 8 (over x, core).
Axes of the slice: x: 4, y: 4, z: 16, core: 2. Of those that a mesh axis runs over, the one named last changes fastest.
Arguments:
- x_resid: bfloat16 [512, 6144], P('exp', 'ctx'), may hold values from -16 to 16
- queries: bfloat16 [512, 6144], P('ctx', 'exp'), may hold values from -5 to 5
- keys: bfloat16 [32768, 1024], P('ctx', 'exp'), may hold values from -4 to 4
- values: bfloat16 [32768, 1024], P('ctx', 'exp'), may hold values from -4 to 4
- pattern: int32 [4, 6], replicated, may hold values from 0 to 254, as said below
- global_blocks: int32 [2], replicated, may hold values from 0 to 248, as said below
- out_weight: bfloat16 [6144, 6144], P('exp', 'ctx'), may hold values from -0.875 to 0.875
- norm_gain: float32 [6144], P('ctx'), may hold values from 0.1 to 1.9
- router: bfloat16 [6144, 8], P('ctx'), may hold values from -0.078125 to 0.078125
- expert_ids: int32 [512, 2], P('exp'), may hold values from 0 to 7, as said below
- expert_slots: int32 [512, 2], P('exp'), may hold values from 0 to 19, as said below
- w_gate: bfloat16 [8, 6144, 8192], P('exp', None, 'ctx'), may hold values from -0.078125 to 0.078125
- w_up: bfloat16 [8, 6144, 8192], P('exp', None, 'ctx'), may hold values from -0.078125 to 0.078125
- w_down: bfloat16 [8, 8192, 6144], P('exp', None, 'ctx'), may hold values from -0.0625 to 0.0625
Outputs:
- layer_out: bfloat16 [512, 6144], P('exp', 'ctx')
Inputs may be any that keep to these rules, and one draw needn't show every extreme that they name: `pattern`: each row lists 3 + 3 different key blocks, none of them a global block. `global_blocks`: 2 different key blocks. `expert_ids`: each token names two different experts; among the tokens of one index of exp (aligned blocks of 64 rows) every expert is named at most 20 times, and one expert, the same in every block, exactly 20 times. `expert_slots`: within one aligned block of 64 rows, the choices that name the same expert have different slots.
All inputs are finite; a program needn't handle non-finite values.
Results may differ from a plain program's by a relative error of at most 0.01.
Values may be sent and summed in bfloat16 or wider, within the bound.
No kernel may reach another device: no remote copies, remote signals or barrier semaphores. Data moves between devices by JAX's collectives and lax.ppermute only.
A program may use at most 64 MiB of HBM per device.

v0:
```python
import jax
import jax.numpy as jnp
from jax import lax
from jax.sharding import PartitionSpec as P

D = 6144
HD = 128
BLK = 128
CAP = 20
eps = 1e-05
masked_score = -1e30


def per_device(
    x_resid,
    queries,
    keys,
    values,
    pattern,
    global_blocks,
    out_weight,
    norm_gain,
    router,
    expert_ids,
    expert_slots,
    w_gate,
    w_up,
    w_down,
):
    all_queries = lax.all_gather(queries, "ctx", axis=0, tiled=True)
    token_count = all_queries.shape[0]
    cache_length = keys.shape[0]
    groups_local = keys.shape[1] // HD
    group = all_queries.shape[1] // HD // groups_local
    query_heads = all_queries.reshape(token_count, groups_local, group, HD)
    key_heads = keys.reshape(cache_length, groups_local, HD)
    value_heads = values.reshape(cache_length, groups_local, HD)
    scores = jnp.einsum(
        "tkgd,pkd->tkgp", query_heads, key_heads, preferred_element_type=jnp.float32
    ) * HD ** (-0.5)
    local_blocks = cache_length // BLK
    block_ids = lax.axis_index("ctx") * local_blocks + jnp.arange(local_blocks, dtype=jnp.int32)
    listed = jnp.any(pattern[:, :, None] == block_ids[None, None, :], axis=1)
    anchored = jnp.any(global_blocks[:, None] == block_ids[None, :], axis=0)
    allowed_blocks = listed | anchored[None, :]
    allowed = jnp.repeat(jnp.repeat(allowed_blocks, BLK, axis=0), BLK, axis=1)[:, None, None, :]
    local_peak = jnp.max(jnp.where(allowed, scores, masked_score), axis=-1)
    peak = lax.pmax(local_peak, "ctx")
    probs = jnp.where(allowed, jnp.exp(scores - peak[..., None]), 0.0).astype(jnp.bfloat16)
    numerator = jnp.einsum("tkgp,pkd->tkgd", probs, value_heads, preferred_element_type=jnp.float32)
    denominator = jnp.sum(probs, axis=-1, dtype=jnp.float32)
    numerator, denominator = lax.psum((numerator, denominator), "ctx")
    attention = (numerator / denominator[..., None]).astype(jnp.bfloat16).reshape(token_count, -1)
    exp_count = lax.axis_size("exp")
    head_total = lax.psum_scatter(
        jnp.dot(attention, out_weight, preferred_element_type=jnp.float32),
        "exp",
        scatter_dimension=0,
        tiled=True,
    )
    residual = x_resid.astype(jnp.float32) + head_total
    scaled = residual * norm_gain
    router_wide = router.astype(jnp.float32)
    squares = lax.psum(jnp.sum(residual * residual, axis=1), "ctx")
    inverse = lax.rsqrt(squares / D + eps)
    logits = lax.psum(
        jnp.dot(scaled * inverse[:, None], router_wide, precision=lax.Precision.HIGHEST), "ctx"
    )
    normed = (scaled * inverse[:, None]).astype(jnp.bfloat16)
    experts_all = router.shape[1]
    onehot = expert_ids[:, :, None] == jnp.arange(experts_all, dtype=jnp.int32)[None, None, :]
    chosen_logits = jnp.sum(jnp.where(onehot, logits[:, None, :], 0.0), axis=-1)
    gate_weights = jax.nn.sigmoid(chosen_logits - chosen_logits[:, ::-1])
    flat_slots = expert_ids * CAP + expert_slots
    positions = jnp.arange(experts_all * CAP, dtype=jnp.int32)
    dispatch = jnp.sum(
        (flat_slots[None, :, :] == positions[:, None, None]).astype(jnp.bfloat16), axis=2
    )
    local_experts = w_gate.shape[0]
    feature_rows = lax.all_gather(normed, "ctx", axis=1, tiled=True)
    outgoing = jnp.dot(dispatch, feature_rows, preferred_element_type=jnp.float32).astype(
        jnp.bfloat16
    )
    outgoing = outgoing.reshape(experts_all, CAP, -1)
    incoming = lax.all_to_all(outgoing, "exp", split_axis=0, concat_axis=0, tiled=True)
    incoming = incoming.reshape(exp_count, local_experts, CAP, -1)
    expert_gate = jnp.einsum("sjcd,jdf->sjcf", incoming, w_gate, preferred_element_type=jnp.float32)
    expert_lift = jnp.einsum("sjcd,jdf->sjcf", incoming, w_up, preferred_element_type=jnp.float32)
    hidden = (jax.nn.silu(expert_gate) * expert_lift).astype(jnp.bfloat16)
    out_width = w_down.shape[2]
    expert_out = jnp.einsum(
        "sjcf,jfd->sjcd",
        lax.all_gather(hidden, "ctx", axis=3, tiled=True),
        w_down,
        preferred_element_type=jnp.float32,
    ).astype(jnp.bfloat16)
    returned = lax.all_to_all(
        expert_out.reshape(experts_all, CAP, out_width),
        "exp",
        split_axis=0,
        concat_axis=0,
        tiled=True,
    )
    picked = jnp.take(returned.reshape(experts_all * CAP, out_width), flat_slots, axis=0).astype(
        jnp.float32
    )
    mixture = jnp.sum(gate_weights[:, :, None] * picked, axis=1)
    return (residual + mixture).astype(jnp.bfloat16)


def solution(mesh):
    in_specs = (
        P("exp", "ctx"),
        P("ctx", "exp"),
        P("ctx", "exp"),
        P("ctx", "exp"),
        P(),
        P(),
        P("exp", "ctx"),
        P("ctx"),
        P("ctx", None),
        P("exp", None),
        P("exp", None),
        P("exp", None, "ctx"),
        P("exp", None, "ctx"),
        P("exp", None, "ctx"),
    )
    out_specs = P("exp", "ctx")
    return jax.shard_map(
        per_device, mesh=mesh, in_specs=in_specs, out_specs=out_specs, check_vma=False
    )
```

profile of v0, /device:TPU:1, one launch (start us, length us, event | category | flops | bytes accessed | tf_op | source)
XLA Modules:
  0.0 1161.9 jit_solution(5624072325766790315)
XLA Ops:
  6.5 0.0 copy-start
  6.5 0.0 all-reduce.2.cloned.1.call-start
  6.5 1.0 compare_reduce_fusion
  7.6 0.8 compare_reduce_fusion.1
  8.3 0.1 copy.41
  8.4 0.1 broadcast_bitcast_fusion
  8.5 82.7 %all_gather.9 = bf16[512,768]{1,0:T(8,128)(2,1)S(1)} all-gather(bf16[8,768]{1,0:T(8,128)(2,1)} %param.15), channel_id=1, replica_groups=mesh['ctx'=64,'exp'=8] {'ctx'}, dimensions={0}, use_global_device_ids=true | all-gather | bytes 798720 | tf_op jit(solution)/shard_map/all_gather | solution.py:30
  91.3 0.3 copy.42
  91.5 0.1 broadcast_in_dim.67
  91.6 0.0 copy-start.16
  91.6 4.8 fusion
  96.4 221.4 %pmax.7 = f32[512,6]{0,1:T(8,128)S(1)} all-reduce(f32[512,6]{0,1:T(8,128)S(1)} %get-tuple-element.7), channel_id=1, replica_groups=mesh['ctx'=64,'exp'=8] {'ctx'}, use_global_device_ids=true, to_apply=%region_3.4 | all-reduce | flops 3072 | bytes 24576 | tf_op jit(solution)/shard_map/pmax | solution.py:48
  317.8 0.0 copy-done.16
  317.8 5.6 fusion.13
  323.4 0.0 all-reduce.2.cloned.1.call-update
  323.4 0.0 reduce-scatter.2.cloned.1.call-start
  323.5 4.1 convert_reduce_fusion
  327.6 0.0 copy-start.4
  327.6 0.0 copy-start.8
  327.6 0.0 copy-start.11
  327.6 0.0 copy-start.5
  327.6 0.0 copy-start.12
  327.6 219.7 %psum.29 = f32[512,6]{0,1:T(8,128)S(1)} all-reduce(f32[512,6]{0,1:T(8,128)S(1)} %convert_reduce_fusion), channel_id=1, replica_groups=mesh['ctx'=64,'exp'=8] {'ctx'}, use_global_device_ids=true, to_apply=%region_6.7 | all-reduce | flops 3072 | bytes 24576 | tf_op jit(solution)/shard_map/psum | solution.py:52
  547.3 113.2 %all-reduce.2.cloned.1.call-done = f32[512,1,6,128]{3,0,2,1:T(8,128)} async-done(((f32[512,1,6,128]{3,0,2,1:T(8,128)}), f32[512,1,6,128]{3,0,2,1:T(8,128)}) %all-reduce.2.cloned.1.call-update) | async-done | bytes 1572880 | tf_op jit(solution)/shard_map/psum | solution.py:52
  660.5 1.9 divide_convert_fusion
  662.4 0.3 copy.45
  662.7 1.1 fusion.44
  663.8 0.0 reduce-scatter.2.cloned.1.call-update
  663.8 0.0 all-gather.3.cloned.1.call-start
  663.9 0.0 copy-done.8
  663.9 0.0 copy-done.11
  663.9 0.6 compare_and_fusion
  664.5 0.6 copy-done.6
  665.0 0.7 fusion.37
  665.7 45.5 %reduce-scatter.2.cloned.1.call-done = f32[64,96]{1,0:T(8,128)} async-done(((f32[512,96]{1,0:T(8,128)}), f32[64,96]{1,0:T(8,128)}) %reduce-scatter.2.cloned.1.call-update) | async-done | bytes 24592 | tf_op jit(solution)/shard_map/reduce_scatter | solution.py:55
  711.2 0.9 multiply_reduce_fusion.1
  712.1 115.6 %psum.30 = f32[64]{0:T(128)S(1)} all-reduce(f32[64]{0:T(128)S(1)} %multiply_reduce_fusion.1), channel_id=1, replica_groups=mesh['ctx'=64,'exp'=8] {'ctx'}, use_global_device_ids=true, to_apply=%region_9.10 | all-reduce | flops 64 | bytes 512 | tf_op jit(solution)/shard_map/psum | solution.py:64
  827.7 0.8 fusion.40
  828.5 72.3 %all-gather = bf16[64,96,64]{1,2,0:T(8,128)(2,1)S(1)} all-gather(bf16[1,96,64]{1,2,0:T(8,128)(2,1)S(1)} %fusion.40), channel_id=1, replica_groups=mesh['ctx'=64,'exp'=8] {'ctx'}, dimensions={0}, use_global_device_ids=true | all-gather | bytes 798720 | tf_op jit(solution)/shard_map/all_gather | solution.py:80
  900.8 0.7 copy.48
  901.5 2.3 reshape.108
  903.8 1.8 convolution_convert_fusion
  905.7 2.1 reshape.89
  907.8 88.6 %all_to_all.10 = bf16[8,20,6144]{2,1,0:T(8,128)(2,1)S(1)} all-to-all(bf16[8,20,6144]{2,1,0:T(8,128)(2,1)} %reshape.89), channel_id=1, replica_groups=mesh['ctx'=64,'exp'=8] {'exp'}, dimensions={0} | all-to-all | bytes 3932160 | tf_op jit(solution)/shard_map/all_to_all | solution.py:85
  996.4 0.0 copy-start.13
  996.5 0.0 copy-start.15
  996.5 0.0 copy-start.17
  996.5 0.8 fusion.16
  997.3 0.6 copy-done.1
  997.8 1.4 fusion.25
  999.2 0.0 all-gather.3.cloned.1.call-update
  999.3 0.1 copy.49
  999.4 0.1 reshape.99
  999.5 0.1 copy.47
  999.7 0.2 fusion.39
  999.9 113.2 %psum.31 = f32[64,8]{0,1:T(8,128)S(1)} all-reduce(f32[64,8]{0,1:T(8,128)S(1)} %fusion.39), channel_id=1, replica_groups=mesh['ctx'=64,'exp'=8] {'ctx'}, use_global_device_ids=true, to_apply=%region_10.11 | all-reduce | flops 512 | bytes 4096 | tf_op jit(solution)/shard_map/psum | solution.py:66
  1113.1 9.4 all-gather.3.cloned.1.call-done
  1122.6 3.5 fusion.28
  1126.1 22.9 %all-to-all-start.1 = ((bf16[8,20,96]{2,1,0:T(8,128)(2,1)}), bf16[8,20,96]{2,1,0:T(8,128)(2,1)S(1)}, u32[]{:S(2)}, u32[]{:S(2)}) async-start(bf16[8,20,96]{2,1,0:T(8,128)(2,1)} %fusion.28), calls=%async_computation.2 | async-start | bytes 98304 | tf_op jit(solution)/shard_map/all_to_all | solution.py:97
  1149.0 0.1 copy.46
  1149.1 4.7 all-to-all-done.1
  1153.8 0.7 gather_fusion
  1154.5 0.2 multiply_reduce_fusion
  1154.7 0.6 add_convert_fusion
  (31 shorter events, 0.2 us)
Async XLA Ops:
  6.5 989.9 %copy-start = (bf16[1,6144,128]{2,1,0:T(8,128)(2,1)S(1)}, bf16[1,6144,128]{2,1,0:T(8,128)(2,1)}, u32[]{:S(2)}) copy-start(bf16[1,6144,128]{2,1,0:T(8,128)(2,1)} %param.25) | copy-start | bytes 4718596
  6.5 654.0 %all-reduce.2.cloned.1.call-start = ((), (), s32[]{:S(2)}) async-start(), calls=%async_computation.3 | async-start | bytes 3145728 | tf_op jit(solution)/shard_map/psum | solution.py:52
  91.6 226.1 %copy-start.16 = (bf16[512,128]{1,0:T(8,128)(2,1)S(1)}, bf16[512,128]{1,0:T(8,128)(2,1)}, u32[]{:S(2)}) copy-start(bf16[512,128]{1,0:T(8,128)(2,1)} %param.17) | copy-start | bytes 393220
  323.4 387.8 %reduce-scatter.2.cloned.1.call-start = ((), (), s32[]{:S(2)}) async-start(), calls=%async_computation.4 | async-start | bytes 294912 | tf_op jit(solution)/shard_map/reduce_scatter | solution.py:55
  327.6 335.1 %copy-start.4 = (bf16[768,96]{0,1:T(8,128)(2,1)S(1)}, bf16[768,96]{0,1:T(8,128)(2,1)}, u32[]{:S(2)}) copy-start(bf16[768,96]{0,1:T(8,128)(2,1)} %param.20) | copy-start | bytes 442372
  327.6 336.3 %copy-start.8 = (s32[64,2]{0,1:T(2,128)S(1)}, s32[64,2]{0,1:T(2,128)}, u32[]{:S(2)}) copy-start(s32[64,2]{0,1:T(2,128)} %param.23) | copy-start | bytes 1540
  327.6 336.3 %copy-start.11 = (s32[64,2]{0,1:T(2,128)S(1)}, s32[64,2]{0,1:T(2,128)}, u32[]{:S(2)}) copy-start(s32[64,2]{0,1:T(2,128)} %param.24) | copy-start | bytes 1540
  327.6 383.6 %copy-start.5 = (bf16[64,96]{1,0:T(8,128)(2,1)S(1)}, bf16[64,96]{1,0:T(8,128)(2,1)}, u32[]{:S(2)}) copy-start(bf16[64,96]{1,0:T(8,128)(2,1)} %param.14) | copy-start | bytes 36868
  327.6 500.0 %copy-start.12 = (f32[96]{0:T(128)S(1)}, f32[96]{0:T(128)}, u32[]{:S(2)}) copy-start(f32[96]{0:T(128)} %param.21) | copy-start | bytes 1156
  663.8 458.7 %all-gather.3.cloned.1.call-start = ((), (), s32[]{:S(2)}) async-start(), calls=%async_computation.5 | async-start | bytes 3194880 | tf_op jit(solution)/shard_map/all_gather | solution.py:93
  664.5 0.6 copy-start.6
  827.7 73.8 %copy-start.14 = (f32[64]{0:T(128)}, f32[64]{0:T(128)S(1)}, u32[]{:S(2)}) copy-start(f32[64]{0:T(128)S(1)} %add_rsqrt_fusion) | copy-start | bytes 772
  996.4 1.4 copy-start.1
  996.4 2.8 copy-start.7
  996.4 3.1 copy-start.10
  996.4 3.2 copy-start.3
  996.4 3.2 copy-start.13
  996.5 3.2 copy-start.15
  996.5 3.2 copy-start.17
  997.8 115.3 %copy-start.9 = (s32[64,2]{0,1:T(2,128)S(1)}, s32[64,2]{0,1:T(2,128)}, u32[]{:S(2)}) copy-start(s32[64,2]{0,1:T(2,128)} %param.23) | copy-start | bytes 1540
  997.8 124.7 %copy-start.2 = (bf16[1,8192,96]{1,2,0:T(8,128)(2,1)S(1)}, bf16[1,8192,96]{1,2,0:T(8,128)(2,1)}, u32[]{:S(2)}) copy-start(bf16[1,8192,96]{1,2,0:T(8,128)(2,1)} %param.27) | copy-start | bytes 4718596
  1126.1 27.7 %all-to-all-start.1 = ((bf16[8,20,96]{2,1,0:T(8,128)(2,1)}), bf16[8,20,96]{2,1,0:T(8,128)(2,1)S(1)}, u32[]{:S(2)}, u32[]{:S(2)}) async-start(bf16[8,20,96]{2,1,0:T(8,128)(2,1)} %fusion.28), calls=%async_computation.2 | async-start | bytes 98304 | tf_op jit(solution)/shard_map/all_to_all | solution.py:97
Sparse Core Ops, SparseCore 0:
  323.6 336.9 all-reduce.1
  664.0 47.1 reduce-scatter.1
  999.4 123.1 all-gather.2
where the time goes:
time: 1160 us
  blocking collectives  914 us (79%)
  waiting for transfers between devices  173 us (15%)
  starting transfers between devices  23 us (2%)
  matrix products  19.2 us (2%)
  between operations  13.4 us (1%)
  other arithmetic  11.6 us (1%)
    pmax x1, blocking collectives, per_device(): peak = lax.pmax(local_peak, 'ctx')  221 us
    psum x1, blocking collectives, per_device(): numerator, denominator = lax.psum((numerator, denominator), 'ctx')  220 us
    psum x1, blocking collectives, per_device(): squares = lax.psum(jnp.sum(residual * residual, axis=1), 'ctx')  116 us
    psum x1, blocking collectives, per_device(): lax.psum(jnp.dot(scaled * inverse[:, None], router_wide, precision=lax.Pr...  113 us
    psum x1, waiting for transfers between devices, per_device(): numerator, denominator = lax.psum((numerator, denominator), 'ctx')  113 us
    all_to_all x1, blocking collectives, per_device(): lax.all_to_all(outgoing, 'exp', split_axis=0, concat_axis=0, tiled=True)  88.6 us
    all_gather x1, blocking collectives, per_device(): all_queries = lax.all_gather(queries, 'ctx', axis=0, tiled=True)  82.7 us
    all_gather x1, blocking collectives, per_device(): feature_rows = lax.all_gather(normed, 'ctx', axis=1, tiled=True)  72.3 us
  transfers between devices with their start and end apart: 4, of which 4 were waited for; matrix products, arithmetic and copies ran while one was open for 1% of the time, Pallas kernels for 0%

commit v1 on v0

--- a/solution.py
+++ b/solution.py
@@ -63,8 +63,11 @@
     router_wide = router.astype(jnp.float32)
     squares = lax.psum(jnp.sum(residual * residual, axis=1), "ctx")
     inverse = lax.rsqrt(squares / D + eps)
-    logits = lax.psum(
-        jnp.dot(scaled * inverse[:, None], router_wide, precision=lax.Precision.HIGHEST), "ctx"
+    logits = jnp.sum(
+        lax.all_gather(
+            jnp.dot(scaled * inverse[:, None], router_wide, precision=lax.Precision.HIGHEST), "ctx"
+        ),
+        axis=0,
     )
     normed = (scaled * inverse[:, None]).astype(jnp.bfloat16)
     experts_all = router.shape[1]

time: 1160 us -> 1150 us (level)
  blocking collectives: 914 us -> 866 us
  waiting for transfers between devices: 173 us -> 220 us
    psum x1 -> x0, blocking collectives: 113 us -> none  [per_device(): lax.psum(jnp.dot(scaled * inverse[:, None], router_wide, precision=lax.Pr...]
    all_gather x0 -> x1, blocking collectives: none -> 65.6 us  [per_device(): lax.all_gather(jnp.dot(scaled * inverse[:, None], router_wide, precision=...]
    all_gather x1, waiting for transfers between devices: 9.44 us -> 56.9 us  [per_device(): lax.all_gather(hidden, 'ctx', axis=3, tiled=True)]
where the time goes in v1:
time: 1150 us
  blocking collectives  866 us (75%)
  waiting for transfers between devices  220 us (19%)
  matrix products  19.2 us (2%)
  starting transfers between devices  14.1 us (1%)
  between operations  13.4 us (1%)
  other arithmetic  11.7 us (1%)
    pmax x1, blocking collectives, per_device(): peak = lax.pmax(local_peak, 'ctx')  221 us
    psum x1, blocking collectives, per_device(): numerator, denominator = lax.psum((numerator, denominator), 'ctx')  220 us
    psum x1, blocking collectives, per_device(): squares = lax.psum(jnp.sum(residual * residual, axis=1), 'ctx')  116 us
    psum x1, waiting for transfers between devices, per_device(): numerator, denominator = lax.psum((numerator, denominator), 'ctx')  113 us
    all_to_all x1, blocking collectives, per_device(): lax.all_to_all(outgoing, 'exp', split_axis=0, concat_axis=0, tiled=True)  88.6 us
    all_gather x1, blocking collectives, per_device(): all_queries = lax.all_gather(queries, 'ctx', axis=0, tiled=True)  82.7 us
    all_gather x1, blocking collectives, per_device(): feature_rows = lax.all_gather(normed, 'ctx', axis=1, tiled=True)  72.3 us
    all_gather x1, blocking collectives, per_device(): lax.all_gather(jnp.dot(scaled * inverse[:, None], router_wide, precision=...  65.6 us
  transfers between devices with their start and end apart: 4, of which 4 were waited for; matrix products, arithmetic and copies ran while one was open for 1% of the time, Pallas kernels for 0%

profile of v1, /device:TPU:1, one launch (start us, length us, event | category | flops | bytes accessed | tf_op | source)
XLA Modules:
  0.0 1152.7 jit_solution(11805528375181506239)
XLA Ops:
  6.5 0.0 copy-start
  6.5 1.0 compare_reduce_fusion
  7.6 0.8 compare_reduce_fusion.1
  8.3 0.1 copy.39
  8.4 0.1 broadcast_bitcast_fusion
  8.5 82.7 %all_gather.15 = bf16[512,768]{1,0:T(8,128)(2,1)S(1)} all-gather(bf16[8,768]{1,0:T(8,128)(2,1)} %param.15), channel_id=1, replica_groups=mesh['ctx'=64,'exp'=8] {'ctx'}, dimensions={0}, use_global_device_ids=true | all-gather | bytes 798720 | tf_op jit(solution)/shard_map/all_gather | solution.py:30
  91.3 0.3 copy.40
  91.5 0.1 broadcast_in_dim.67
  91.6 0.0 copy-start.16
  91.6 4.8 fusion
  96.4 221.4 %pmax.7 = f32[512,6]{0,1:T(8,128)S(1)} all-reduce(f32[512,6]{0,1:T(8,128)S(1)} %get-tuple-element.7), channel_id=1, replica_groups=mesh['ctx'=64,'exp'=8] {'ctx'}, use_global_device_ids=true, to_apply=%region_3.4 | all-reduce | flops 3072 | bytes 24576 | tf_op jit(solution)/shard_map/pmax | solution.py:48
  317.8 5.6 fusion.13
  323.4 0.0 all-reduce.2.cloned.1.call-update
  323.4 0.0 reduce-scatter.2.cloned.1.call-start
  323.5 4.1 convert_reduce_fusion
  327.6 0.0 copy-start.4
  327.6 0.0 copy-start.8
  327.6 0.0 copy-start.11
  327.6 0.0 copy-start.5
  327.6 0.0 copy-start.12
  327.6 219.7 %psum.22 = f32[512,6]{0,1:T(8,128)S(1)} all-reduce(f32[512,6]{0,1:T(8,128)S(1)} %convert_reduce_fusion), channel_id=1, replica_groups=mesh['ctx'=64,'exp'=8] {'ctx'}, use_global_device_ids=true, to_apply=%region_6.7 | all-reduce | flops 3072 | bytes 24576 | tf_op jit(solution)/shard_map/psum | solution.py:52
  547.3 113.2 %all-reduce.2.cloned.1.call-done = f32[512,1,6,128]{3,0,2,1:T(8,128)} async-done(((f32[512,1,6,128]{3,0,2,1:T(8,128)}), f32[512,1,6,128]{3,0,2,1:T(8,128)}) %all-reduce.2.cloned.1.call-update) | async-done | bytes 1572880 | tf_op jit(solution)/shard_map/psum | solution.py:52
  660.5 1.9 divide_convert_fusion
  662.4 0.3 copy.43
  662.7 1.1 fusion.43
  663.8 0.0 reduce-scatter.2.cloned.1.call-update
  663.8 0.0 all-gather.5.cloned.1.call-start
  663.9 0.0 copy-done.8
  663.9 0.0 copy-done.11
  663.9 0.6 compare_and_fusion
  664.5 0.6 copy-done.6
  665.0 0.7 fusion.37
  665.7 45.5 %reduce-scatter.2.cloned.1.call-done = f32[64,96]{1,0:T(8,128)} async-done(((f32[512,96]{1,0:T(8,128)}), f32[64,96]{1,0:T(8,128)}) %reduce-scatter.2.cloned.1.call-update) | async-done | bytes 24592 | tf_op jit(solution)/shard_map/reduce_scatter | solution.py:55
  711.2 0.9 multiply_reduce_fusion.1
  712.1 115.6 %psum.23 = f32[64]{0:T(128)S(1)} all-reduce(f32[64]{0:T(128)S(1)} %multiply_reduce_fusion.1), channel_id=1, replica_groups=mesh['ctx'=64,'exp'=8] {'ctx'}, use_global_device_ids=true, to_apply=%region_9.10 | all-reduce | flops 64 | bytes 512 | tf_op jit(solution)/shard_map/psum | solution.py:64
  827.7 0.8 fusion.39
  828.5 72.3 %all-gather.2 = bf16[64,96,64]{1,2,0:T(8,128)(2,1)S(1)} all-gather(bf16[1,96,64]{1,2,0:T(8,128)(2,1)S(1)} %fusion.39), channel_id=1, replica_groups=mesh['ctx'=64,'exp'=8] {'ctx'}, dimensions={0}, use_global_device_ids=true | all-gather | bytes 798720 | tf_op jit(solution)/shard_map/all_gather | solution.py:83
  900.8 0.7 copy.46
  901.5 2.3 reshape.111
  903.8 1.8 convolution_convert_fusion
  905.7 2.1 reshape.89
  907.8 88.6 %all_to_all.10 = bf16[8,20,6144]{2,1,0:T(8,128)(2,1)S(1)} all-to-all(bf16[8,20,6144]{2,1,0:T(8,128)(2,1)} %reshape.89), channel_id=1, replica_groups=mesh['ctx'=64,'exp'=8] {'exp'}, dimensions={0} | all-to-all | bytes 3932160 | tf_op jit(solution)/shard_map/all_to_all | solution.py:88
  996.4 0.0 copy-start.13
  996.5 0.0 copy-start.15
  996.5 0.0 copy-start.17
  996.5 0.8 fusion.16
  997.3 0.6 copy-done.1
  997.8 1.4 fusion.25
  999.2 0.0 all-gather.5.cloned.1.call-update
  999.3 0.1 copy.47
  999.4 0.1 reshape.99
  999.5 0.1 copy.45
  999.7 0.2 convolution_bitcast_fusion
  999.9 65.6 %all-gather.1 = f32[64,64,8]{1,2,0:T(8,128)S(1)} all-gather(f32[1,64,8]{1,2,0:T(8,128)S(1)} %convolution_bitcast_fusion), channel_id=2, replica_groups=mesh['ctx'=64,'exp'=8] {'ctx'}, dimensions={0}, use_global_device_ids=true | all-gather | bytes 133120 | tf_op jit(solution)/shard_map/all_gather | solution.py:67
  1065.4 0.1 reduce_sum.62
  1065.5 0.0 copy-done.9
  1065.5 56.9 %all-gather.5.cloned.1.call-done = bf16[8,1,20,8192]{3,2,0,1:T(8,128)(2,1)} async-done(((bf16[8,1,20,128]{3,2,0,1:T(8,128)(2,1)}), bf16[8,1,20,8192]{3,2,0,1:T(8,128)(2,1)}) %all-gather.5.cloned.1.call-update) | async-done | bytes 2621456 | tf_op jit(solution)/shard_map/all_gather | solution.py:96
  1122.4 3.5 fusion.28
  1125.9 14.0 %all-to-all-start.1 = ((bf16[8,20,96]{2,1,0:T(8,128)(2,1)}), bf16[8,20,96]{2,1,0:T(8,128)(2,1)S(1)}, u32[]{:S(2)}, u32[]{:S(2)}) async-start(bf16[8,20,96]{2,1,0:T(8,128)(2,1)} %fusion.28), calls=%async_computation.2 | async-start | bytes 98304 | tf_op jit(solution)/shard_map/all_to_all | solution.py:100
  1139.9 0.1 copy.44
  1140.0 4.7 all-to-all-done.1
  1144.7 0.7 gather_fusion
  1145.4 0.2 multiply_reduce_fusion
  1145.6 0.6 add_convert_fusion
  (32 shorter events, 0.2 us)
Async XLA Ops:
  6.5 989.9 %copy-start = (bf16[1,6144,128]{2,1,0:T(8,128)(2,1)S(1)}, bf16[1,6144,128]{2,1,0:T(8,128)(2,1)}, u32[]{:S(2)}) copy-start(bf16[1,6144,128]{2,1,0:T(8,128)(2,1)} %param.25) | copy-start | bytes 4718596
  6.5 654.0 %all-reduce.2.cloned.1.call-start = ((), (), s32[]{:S(2)}) async-start(), calls=%async_computation.3 | async-start | bytes 3145728 | tf_op jit(solution)/shard_map/psum | solution.py:52
  91.6 226.1 %copy-start.16 = (bf16[512,128]{1,0:T(8,128)(2,1)S(1)}, bf16[512,128]{1,0:T(8,128)(2,1)}, u32[]{:S(2)}) copy-start(bf16[512,128]{1,0:T(8,128)(2,1)} %param.17) | copy-start | bytes 393220
  323.4 387.8 %reduce-scatter.2.cloned.1.call-start = ((), (), s32[]{:S(2)}) async-start(), calls=%async_computation.4 | async-start | bytes 294912 | tf_op jit(solution)/shard_map/reduce_scatter | solution.py:55
  327.6 335.1 %copy-start.4 = (bf16[768,96]{0,1:T(8,128)(2,1)S(1)}, bf16[768,96]{0,1:T(8,128)(2,1)}, u32[]{:S(2)}) copy-start(bf16[768,96]{0,1:T(8,128)(2,1)} %param.20) | copy-start | bytes 442372
  327.6 336.3 %copy-start.8 = (s32[64,2]{0,1:T(2,128)S(1)}, s32[64,2]{0,1:T(2,128)}, u32[]{:S(2)}) copy-start(s32[64,2]{0,1:T(2,128)} %param.23) | copy-start | bytes 1540
  327.6 336.3 %copy-start.11 = (s32[64,2]{0,1:T(2,128)S(1)}, s32[64,2]{0,1:T(2,128)}, u32[]{:S(2)}) copy-start(s32[64,2]{0,1:T(2,128)} %param.24) | copy-start | bytes 1540
  327.6 383.6 %copy-start.5 = (bf16[64,96]{1,0:T(8,128)(2,1)S(1)}, bf16[64,96]{1,0:T(8,128)(2,1)}, u32[]{:S(2)}) copy-start(bf16[64,96]{1,0:T(8,128)(2,1)} %param.14) | copy-start | bytes 36868
  327.6 500.0 %copy-start.12 = (f32[96]{0:T(128)S(1)}, f32[96]{0:T(128)}, u32[]{:S(2)}) copy-start(f32[96]{0:T(128)} %param.21) | copy-start | bytes 1156
  663.8 458.6 %all-gather.5.cloned.1.call-start = ((), (), s32[]{:S(2)}) async-start(), calls=%async_computation.5 | async-start | bytes 3194880 | tf_op jit(solution)/shard_map/all_gather | solution.py:96
  664.5 0.6 copy-start.6
  827.7 73.8 %copy-start.14 = (f32[64]{0:T(128)}, f32[64]{0:T(128)S(1)}, u32[]{:S(2)}) copy-start(f32[64]{0:T(128)S(1)} %add_rsqrt_fusion) | copy-start | bytes 772
  996.4 1.4 copy-start.1
  996.4 2.8 copy-start.7
  996.4 3.1 copy-start.10
  996.4 3.2 copy-start.3
  996.4 3.2 copy-start.13
  996.5 3.2 copy-start.15
  996.5 3.2 copy-start.17
  997.8 67.7 %copy-start.9 = (s32[64,2]{0,1:T(2,128)S(1)}, s32[64,2]{0,1:T(2,128)}, u32[]{:S(2)}) copy-start(s32[64,2]{0,1:T(2,128)} %param.23) | copy-start | bytes 1540
  997.8 124.6 %copy-start.2 = (bf16[1,8192,96]{1,2,0:T(8,128)(2,1)S(1)}, bf16[1,8192,96]{1,2,0:T(8,128)(2,1)}, u32[]{:S(2)}) copy-start(bf16[1,8192,96]{1,2,0:T(8,128)(2,1)} %param.27) | copy-start | bytes 4718596
  1125.9 18.8 %all-to-all-start.1 = ((bf16[8,20,96]{2,1,0:T(8,128)(2,1)}), bf16[8,20,96]{2,1,0:T(8,128)(2,1)S(1)}, u32[]{:S(2)}, u32[]{:S(2)}) async-start(bf16[8,20,96]{2,1,0:T(8,128)(2,1)} %fusion.28), calls=%async_computation.2 | async-start | bytes 98304 | tf_op jit(solution)/shard_map/all_to_all | solution.py:100
Sparse Core Ops, SparseCore 0:
  323.6 336.9 all-reduce.1
  664.0 47.1 reduce-scatter.1
  999.4 122.9 all-gather.4
